TPU v7x, 32 devices: a whole 2x2x4 slice. The times are simulated.
32 devices in a mesh: dp: 8 (over z, core), blk: 4 (over y, x).
Axes of the slice: x: 2, y: 2, z: 4, core: 2. Of those that a mesh axis runs over, the one named last changes fastest.
Arguments:
- tokens: bfloat16 [8, 2048, 1024], P('dp', 'blk'), may hold values from -6 to 6
- cotangent: bfloat16 [8, 2048, 1024], P('dp', 'blk'), may hold values from -6 to 6
- lengths: int32 [8, 16], P('dp'), may hold values from 0 to 2048, as said below
- w_query: bfloat16 [1024, 1024], replicated, may hold values from -0.1875 to 0.1875
- w_key: bfloat16 [1024, 1024], replicated, may hold values from -0.1875 to 0.1875
- w_value: bfloat16 [1024, 1024], replicated, may hold values from -0.1875 to 0.1875
- w_out: bfloat16 [1024, 1024], replicated, may hold values from -0.1875 to 0.1875
- w_up: bfloat16 [1024, 4096], replicated, may hold values from -0.1875 to 0.1875
- w_down: bfloat16 [4096, 1024], replicated, may hold values from -0.09375 to 0.09375
- norm_gain: float32 [4, 1024], replicated, may hold values from 0.1 to 1.9
- norm_bias: float32 [4, 1024], replicated, may hold values from -1.8 to 1.8
Outputs:
- mixed: bfloat16 [8, 2048, 1024], P('dp', 'blk')
- grad_tokens: bfloat16 [8, 2048, 1024], P('dp', 'blk')
- grad_query: float32 [1024, 1024], replicated
- grad_key: float32 [1024, 1024], replicated
- grad_value: float32 [1024, 1024], replicated
- grad_out: float32 [1024, 1024], replicated
- grad_up: float32 [1024, 4096], replicated
- grad_down: float32 [4096, 1024], replicated
- grad_gain: float32 [4, 1024], replicated
- grad_bias: float32 [4, 1024], replicated
Inputs may be any that keep to these rules, and one draw needn't show every extreme that they name: `lengths`: A row holds its sequences one after another from slot 0 in the order of its entries, zero entries are unused, every other entry is 128 or more, and the slots after them are padding. Of every four consecutive rows exactly one is a single sequence of 2048 tokens; each other row holds at most 1536 real tokens.
All inputs are finite; a program needn't handle non-finite values.
Results may differ from a plain program's by a relative error of at most 0.02.
Values may be sent and summed in bfloat16 or wider, within the bound.
A program may use at most 256 MiB of HBM per device.

v0:
```python
import jax
import jax.numpy as jnp
from jax import lax
from jax.sharding import PartitionSpec as P

HEAD = 64


EPSILON = 1e-05
MASKED_SCORE = -1e30


def passed_along(value, axis, steps):
    count = lax.axis_size(axis)
    pairs = [(source, (source + steps) % count) for source in range(count)]
    return lax.ppermute(value, axis, pairs)


def normalize(values, norm_scale, norm_shift):
    row_mean = jnp.mean(values, axis=-1, keepdims=True)
    centred = values - row_mean
    spread = jnp.mean(centred * centred, axis=-1, keepdims=True)
    return centred * lax.rsqrt(spread + EPSILON) * norm_scale + norm_shift


def rotate(values, position):
    head_count = values.shape[-1] // HEAD
    shaped = values.reshape(values.shape[:-1] + (head_count, HEAD))
    half_len = HEAD // 2
    frequency = jnp.exp(-jnp.log(10000.0) * jnp.arange(half_len, dtype=jnp.float32) * 2.0 / HEAD)
    angles = position.astype(jnp.float32)[..., None] * frequency
    cos_part = jnp.cos(angles)[..., None, :]
    sin_part = jnp.sin(angles)[..., None, :]
    first_half = shaped[..., :half_len]
    second_half = shaped[..., half_len:]
    turned = jnp.concatenate(
        [
            first_half * cos_part - second_half * sin_part,
            second_half * cos_part + first_half * sin_part,
        ],
        axis=-1,
    )
    return turned.reshape(values.shape)


def layout(seg_ends, slot_ids):
    passed = slot_ids[None, :, None] >= seg_ends[:, None, :]
    segment = jnp.sum(passed.astype(jnp.int32), axis=-1)
    seg_start = jnp.max(jnp.where(passed, seg_ends[:, None, :], 0), axis=-1)
    return (segment, slot_ids[None, :] - seg_start, slot_ids[None, :] < seg_ends[:, -1:])


def product(left, right):
    return jnp.dot(left, right, preferred_element_type=jnp.float32)


def contract_rows(left, right):
    return lax.dot_general(
        left, right, (((0,), (0,)), ((), ())), preferred_element_type=jnp.float32
    )


def contract_cols(left, right):
    return lax.dot_general(
        left, right, (((1,), (1,)), ((), ())), preferred_element_type=jnp.float32
    )


def shards(
    tokens, cotangent, lengths, w_query, w_key, w_value, w_out, w_up, w_down, norm_gain, norm_bias
):
    row_count, block_len, model_width = tokens.shape
    head_count = model_width // HEAD
    cycle_size = lax.axis_size("blk")
    cycle_index = lax.axis_index("blk")
    score_scale = HEAD ** (-0.5)
    seg_ends = jnp.cumsum(lengths, axis=1)
    offsets = jnp.arange(block_len, dtype=jnp.int32)
    query_slots = cycle_index * block_len + offsets
    query_segment, query_position, valid_mask = layout(seg_ends, query_slots)
    positions = query_position.reshape(-1)
    valid_col = valid_mask.reshape(-1, 1).astype(jnp.float32)
    inputs = tokens.astype(jnp.float32).reshape(-1, model_width)
    normed, first_back = jax.vjp(normalize, inputs, norm_gain[0], norm_bias[0])
    normed_low = normed.astype(jnp.bfloat16)
    query_full, turn_back = jax.vjp(
        lambda values: rotate(values, positions), product(normed_low, w_query)
    )
    key_full = rotate(product(normed_low, w_key), positions)
    query_low = query_full.astype(jnp.bfloat16).reshape(row_count, block_len, head_count, HEAD)
    key_value = jnp.stack(
        [key_full.astype(jnp.bfloat16), product(normed_low, w_value).astype(jnp.bfloat16)]
    ).reshape(2, row_count, block_len, model_width)

    def needed_for(source):
        key_segment = layout(seg_ends, source * block_len + offsets)[0]
        earlier = source <= cycle_index
        return earlier & jnp.any(key_segment[:, -1] >= query_segment[:, 0])

    def block_scores(key_rows, source):
        key_slots = source * block_len + offsets
        key_segment = layout(seg_ends, key_slots)[0]
        allowed = (key_slots[None, None, :] <= query_slots[None, :, None]) & (
            key_segment[:, None, :] == query_segment[:, :, None]
        )
        key_heads = key_rows.reshape(row_count, block_len, head_count, HEAD)
        scores = (
            jnp.einsum("rqhd,rkhd->rhqk", query_low, key_heads, preferred_element_type=jnp.float32)
            * score_scale
        )
        return (scores, allowed[:, None])

    def absorb(running, block_pair, source):

        def absorb_compute(held):
            run_max, run_sum, run_out = held
            scores, allowed = block_scores(block_pair[0], source)
            masked = jnp.where(allowed, scores, MASKED_SCORE)
            new_max = jnp.maximum(run_max, jnp.max(masked, axis=-1))
            raised = jnp.where(allowed, jnp.exp(masked - new_max[..., None]), 0.0)
            decays = jnp.exp(run_max - new_max)
            value_heads = block_pair[1].reshape(row_count, block_len, head_count, HEAD)
            update = jnp.einsum(
                "rhqk,rkhd->rqhd",
                raised.astype(jnp.bfloat16),
                value_heads,
                preferred_element_type=jnp.float32,
            )
            run_out = run_out * jnp.swapaxes(decays, 1, 2)[..., None] + update
            return (new_max, run_sum * decays + jnp.sum(raised, axis=-1), run_out)

        return lax.cond(needed_for(source), absorb_compute, lambda carried: carried, running)

    starting = (
        jnp.full((row_count, head_count, block_len), MASKED_SCORE, jnp.float32),
        jnp.zeros((row_count, head_count, block_len), jnp.float32),
        jnp.zeros((row_count, block_len, head_count, HEAD), jnp.float32),
    )
    running = absorb(starting, key_value, cycle_index)

    def forward_hop(hop, carried):
        state_now, visiting = carried
        visiting = passed_along(visiting, "blk", -1)
        return (absorb(state_now, visiting, jnp.mod(cycle_index + hop, cycle_size)), visiting)

    running, visited = lax.fori_loop(1, cycle_size, forward_hop, (running, key_value))
    run_max, run_sum, run_out = running
    attended_full = run_out / jnp.swapaxes(run_sum, 1, 2)[..., None]
    log_total = run_max + jnp.log(run_sum)
    attended_low = attended_full.astype(jnp.bfloat16).reshape(-1, model_width)
    post_norm, second_back = jax.vjp(
        normalize, product(attended_low, w_out), norm_gain[1], norm_bias[1]
    )
    hidden = inputs + post_norm
    inner_norm, third_back = jax.vjp(normalize, hidden, norm_gain[2], norm_bias[2])
    inner_low = inner_norm.astype(jnp.bfloat16)
    active, gelu_back = jax.vjp(jax.nn.gelu, product(inner_low, w_up))
    active_low = active.astype(jnp.bfloat16)
    outer_norm, fourth_back = jax.vjp(
        normalize, product(active_low, w_down), norm_gain[3], norm_bias[3]
    )
    mixed = ((hidden + outer_norm) * valid_col).astype(jnp.bfloat16).reshape(tokens.shape)
    grad_rows = cotangent.astype(jnp.float32).reshape(-1, model_width) * valid_col
    down_grad, gain_fourth, bias_fourth = fourth_back(grad_rows)
    down_low = down_grad.astype(jnp.bfloat16)
    grad_down_weight = contract_rows(active_low, down_low)
    up_grad = gelu_back(contract_cols(down_low, w_down))[0]
    up_low = up_grad.astype(jnp.bfloat16)
    grad_up_weight = contract_rows(inner_low, up_low)
    inner_grad, gain_third, bias_third = third_back(contract_cols(up_low, w_up))
    hidden_grad = grad_rows + inner_grad
    late_norms = jnp.concatenate([gain_third, gain_fourth, bias_third, bias_fourth])
    proj_grad, gain_second, bias_second = second_back(hidden_grad)
    proj_low = proj_grad.astype(jnp.bfloat16)
    grad_out_weight = contract_rows(attended_low, proj_low)
    attended_grad = (
        contract_cols(proj_low, w_out)
        .astype(jnp.bfloat16)
        .reshape(row_count, block_len, head_count, HEAD)
    )
    delta_rows = jnp.swapaxes(
        jnp.sum(attended_grad.astype(jnp.float32) * attended_full, axis=-1), 1, 2
    )

    def reflect(held, block_pair, source):

        def reflect_compute(inside):
            query_acc, pair_grads = inside
            scores, allowed = block_scores(block_pair[0], source)
            weights = jnp.where(
                allowed,
                jnp.exp(jnp.where(allowed, scores, MASKED_SCORE) - log_total[..., None]),
                0.0,
            )
            key_heads = block_pair[0].reshape(row_count, block_len, head_count, HEAD)
            value_heads = block_pair[1].reshape(row_count, block_len, head_count, HEAD)
            weight_grads = jnp.einsum(
                "rqhd,rkhd->rhqk", attended_grad, value_heads, preferred_element_type=jnp.float32
            )
            score_grads = (weights * (weight_grads - delta_rows[..., None])).astype(jnp.bfloat16)
            query_acc = (
                query_acc
                + jnp.einsum(
                    "rhqk,rkhd->rqhd", score_grads, key_heads, preferred_element_type=jnp.float32
                )
                * score_scale
            )
            key_part = (
                jnp.einsum(
                    "rhqk,rqhd->rkhd", score_grads, query_low, preferred_element_type=jnp.float32
                )
                * score_scale
            )
            value_part = jnp.einsum(
                "rhqk,rqhd->rkhd",
                weights.astype(jnp.bfloat16),
                attended_grad,
                preferred_element_type=jnp.float32,
            )
            pair_grads = pair_grads + jnp.stack([key_part, value_part]).reshape(pair_grads.shape)
            return (query_acc, pair_grads)

        return lax.cond(needed_for(source), reflect_compute, lambda carried: carried, held)

    query_start = jnp.zeros((row_count, block_len, head_count, HEAD), jnp.float32)
    pair_start = jnp.zeros((2, row_count, block_len, model_width), jnp.float32)

    def send_grads(pair_grads):
        return passed_along(pair_grads.astype(jnp.bfloat16), "blk", -1).astype(pair_grads.dtype)

    def backward_hop(hop, carried):
        query_acc, pair_grads, visiting = carried
        query_acc, pair_grads = reflect(
            (query_acc, pair_grads), visiting, jnp.mod(cycle_index + hop, cycle_size)
        )
        visiting = passed_along(visiting, "blk", -1)
        return (query_acc, send_grads(pair_grads), visiting)

    query_acc, pair_grads, visiting = lax.fori_loop(
        0, cycle_size - 1, backward_hop, (query_start, pair_start, key_value)
    )
    query_acc, pair_grads = reflect(
        (query_acc, pair_grads), visiting, jnp.mod(cycle_index - 1, cycle_size)
    )
    own_grads = send_grads(pair_grads)
    query_grad = turn_back(query_acc.reshape(-1, model_width))[0].astype(jnp.bfloat16)
    key_grad = turn_back(own_grads[0].reshape(-1, model_width))[0].astype(jnp.bfloat16)
    value_grad = own_grads[1].reshape(-1, model_width).astype(jnp.bfloat16)
    grad_query_weight = contract_rows(normed_low, query_grad)
    grad_key_weight = contract_rows(normed_low, key_grad)
    grad_value_weight = contract_rows(normed_low, value_grad)
    normed_grad = (
        contract_cols(query_grad, w_query)
        + contract_cols(key_grad, w_key)
        + contract_cols(value_grad, w_value)
    )
    input_grad, gain_first, bias_first = first_back(normed_grad)
    grad_tokens = (hidden_grad + input_grad).astype(jnp.bfloat16).reshape(tokens.shape)
    early_norms = jnp.concatenate([gain_first, gain_second, bias_first, bias_second])
    shares = (
        lax.psum_scatter(
            grad_query_weight.reshape(-1), ("dp", "blk"), scatter_dimension=0, tiled=True
        ),
        lax.psum_scatter(
            grad_key_weight.reshape(-1), ("dp", "blk"), scatter_dimension=0, tiled=True
        ),
        lax.psum_scatter(
            grad_value_weight.reshape(-1), ("dp", "blk"), scatter_dimension=0, tiled=True
        ),
        lax.psum_scatter(
            grad_out_weight.reshape(-1), ("dp", "blk"), scatter_dimension=0, tiled=True
        ),
        lax.psum_scatter(early_norms, ("dp", "blk"), scatter_dimension=0, tiled=True),
        lax.psum_scatter(
            grad_up_weight.reshape(-1), ("dp", "blk"), scatter_dimension=0, tiled=True
        ),
        lax.psum_scatter(
            grad_down_weight.reshape(-1), ("dp", "blk"), scatter_dimension=0, tiled=True
        ),
        lax.psum_scatter(late_norms, ("dp", "blk"), scatter_dimension=0, tiled=True),
    )
    summed = (
        lax.all_gather(shares[0].astype(jnp.bfloat16), ("dp", "blk"), axis=0, tiled=True).astype(
            jnp.float32
        ),
        lax.all_gather(shares[1].astype(jnp.bfloat16), ("dp", "blk"), axis=0, tiled=True).astype(
            jnp.float32
        ),
        lax.all_gather(shares[2].astype(jnp.bfloat16), ("dp", "blk"), axis=0, tiled=True).astype(
            jnp.float32
        ),
        lax.all_gather(shares[3].astype(jnp.bfloat16), ("dp", "blk"), axis=0, tiled=True).astype(
            jnp.float32
        ),
        lax.all_gather(shares[4].astype(jnp.bfloat16), ("dp", "blk"), axis=0, tiled=True).astype(
            jnp.float32
        ),
        lax.all_gather(shares[5].astype(jnp.bfloat16), ("dp", "blk"), axis=0, tiled=True).astype(
            jnp.float32
        ),
        lax.all_gather(shares[6].astype(jnp.bfloat16), ("dp", "blk"), axis=0, tiled=True).astype(
            jnp.float32
        ),
        lax.all_gather(shares[7].astype(jnp.bfloat16), ("dp", "blk"), axis=0, tiled=True).astype(
            jnp.float32
        ),
    )
    square_shape = (model_width, model_width)
    norm_early = summed[4].reshape(4, model_width)
    norm_late = summed[7].reshape(4, model_width)
    grad_gain = jnp.stack([norm_early[0], norm_early[1], norm_late[0], norm_late[1]])
    grad_bias = jnp.stack([norm_early[2], norm_early[3], norm_late[2], norm_late[3]])
    return (
        mixed,
        grad_tokens,
        summed[0].reshape(square_shape),
        summed[1].reshape(square_shape),
        summed[2].reshape(square_shape),
        summed[3].reshape(square_shape),
        summed[5].reshape(model_width, -1),
        summed[6].reshape(-1, model_width),
        grad_gain,
        grad_bias,
    )


def solution(mesh):
    return jax.shard_map(
        shards,
        mesh=mesh,
        in_specs=(
            P("dp", "blk", None),
            P("dp", "blk", None),
            P("dp", None),
            P(),
            P(),
            P(),
            P(),
            P(),
            P(),
            P(),
            P(),
        ),
        out_specs=(
            P("dp", "blk", None),
            P("dp", "blk", None),
            P(),
            P(),
            P(),
            P(),
            P(),
            P(),
            P(),
            P(),
        ),
        check_vma=False,
    )
```

profile of v0, /device:TPU:0, one launch (start us, length us, event | category | flops | bytes accessed | tf_op | source)
XLA Modules:
  0.0 2066.2 jit_solution(14045530810109099162)
XLA Ops:
  14.2 4.0 copy.53
  19.0 3.9 copy.52
  36.5 3.9 copy.56
  43.7 19.1 conditional.4
  44.3 3.9 copy.55
  49.9 3.4 fusion.8
  53.3 4.0 fusion.10
  57.4 5.3 bitcast_add_fusion
  62.8 152.8 %while.44 = (s32[]{:T(128)}, f32[1,16,512]{2,1,0:T(8,128)S(1)}, f32[1,16,512]{2,1,0:T(8,128)S(1)}, f32[1,512,16,64]{1,3,2,0:T(8,128)}, bf16[2,1,512,1024]{2,3,1,...) while((s32[]{:T(128)}, f32[1,16,512]{2,1,0:T(8,128)S(1)}, ...), condition=%wide.region_17.18_spmd.clone.clone, body=%wide.region_10.17_spmd.clone.clone.sunk | while | flops 1130177024 | bytes 80245416 | solution.py:146
  62.8 3.9 collective-permute-start
  69.3 42.7 %collective-permute-done = bf16[2,1,512,1024]{2,3,1,0:T(8,128)(2,1)} collective-permute-done((bf16[2,1,512,1024]{2,3,1,0:T(8,128)(2,1)}, bf16[2,1,512,1024]{2,3,1,0:T(8,128)(2,1)}, u32[]{:S(2)}, u32[]{:S(2)}) %collective-permute-start) | collective-permute-done | bytes 2097184 | tf_op jit(solution)/shard_map/while/body/eval_jaxpr/ppermute | solution.py:16
  115.0 3.4 collective-permute-start
  120.9 41.8 %collective-permute-done = bf16[2,1,512,1024]{2,3,1,0:T(8,128)(2,1)} collective-permute-done((bf16[2,1,512,1024]{2,3,1,0:T(8,128)(2,1)}, bf16[2,1,512,1024]{2,3,1,0:T(8,128)(2,1)}, u32[]{:S(2)}, u32[]{:S(2)}) %collective-permute-start) | collective-permute-done | bytes 2097184 | tf_op jit(solution)/shard_map/while/body/eval_jaxpr/ppermute | solution.py:16
  165.8 3.4 collective-permute-start
  171.7 40.9 %collective-permute-done = bf16[2,1,512,1024]{2,3,1,0:T(8,128)(2,1)} collective-permute-done((bf16[2,1,512,1024]{2,3,1,0:T(8,128)(2,1)}, bf16[2,1,512,1024]{2,3,1,0:T(8,128)(2,1)}, u32[]{:S(2)}, u32[]{:S(2)}) %collective-permute-start) | collective-permute-done | bytes 2097184 | tf_op jit(solution)/shard_map/while/body/eval_jaxpr/ppermute | solution.py:16
  222.9 7.6 fusion.126
  230.5 3.4 copy-done.73
  233.9 8.7 fusion.148
  247.5 15.6 fusion.68
  263.1 9.4 multiply_reduce_fusion
  286.1 365.5 %while.45 = (s32[]{:T(128)}, f32[1,512,16,64]{1,3,2,0:T(8,128)}, f32[2,1,512,1024]{2,3,1,0:T(8,128)}, bf16[2,1,512,1024]{2,3,1,0:T(8,128)(2,1)}, s32[]{:T(128)},...) while((s32[]{:T(128)}, f32[1,512,16,64]{1,3,2,0:T(8,128)}, ...), condition=%wide.region_37.38_spmd.clone.clone, body=%wide.region_32.37_spmd.clone.clone.sunk | while | flops 2742338048 | bytes 176026352 | solution.py:239
  294.6 41.6 %conditional.13 = ((f32[1,512,16,64]{1,3,2,0:T(8,128)}, f32[2,1,512,1024]{2,3,1,0:T(8,128)})) conditional(s32[]{:T(128)} %convert_element_type.561, (f32[1,512,16,64]{1,3,2,0:T(8,128)}, f32[2,1,512,1024]{2,3,1,0:T(8,128)}) %tuple.233, (s32[]{:T(128)}, s32[512]{0:T(512)S(1)}, s32[]{:T(128)}, s32[1,16]{1,0:T(1,128)S(1)}, s32[1,512]{1,0:T(1,128)S(1)}, ...), branch_computations={%region_34.34_spmd, %region_35.36_spmd} | conditional | flops 2739167744 | bytes 108908648 | solution.py:223
  296.3 8.5 fusion.44
  305.2 10.3 multiply_convert_fusion
  315.5 5.5 bitcast_add_fusion.4
  321.1 8.5 fusion.38
  331.0 5.2 maximum_add_fusion
  336.2 3.9 convert_element_type.562
  340.1 20.6 collective-permute-start.1
  360.7 46.4 %collective-permute-done.1 = bf16[2,1,512,1024]{2,3,1,0:T(8,128)(2,1)} collective-permute-done((bf16[2,1,512,1024]{2,3,1,0:T(8,128)(2,1)}, bf16[2,1,512,1024]{2,3,1,0:T(8,128)(2,1)}, u32[]{:S(2)}, u32[]{:S(2)}) %collective-permute-start.1) | collective-permute-done | bytes 2097184 | tf_op jit(solution)/shard_map/while/body/eval_jaxpr/ppermute | solution.py:16
  407.1 4.2 convert_element_type.563
  411.3 36.7 %collective-permute-done.2 = bf16[2,1,512,1024]{2,3,1,0:T(8,128)(2,1)} collective-permute-done((bf16[2,1,512,1024]{2,3,1,0:T(8,128)(2,1)S(1)}, bf16[2,1,512,1024]{2,3,1,0:T(8,128)(2,1)}, u32[]{:S(2)}, u32[]{:S(2)}) %collective-permute-start.2) | collective-permute-done | bytes 2097184 | tf_op jit(solution)/shard_map/while/body/eval_jaxpr/ppermute | solution.py:16
  456.4 3.9 convert_element_type.562
  460.3 3.5 collective-permute-start.1
  463.8 46.4 %collective-permute-done.1 = bf16[2,1,512,1024]{2,3,1,0:T(8,128)(2,1)} collective-permute-done((bf16[2,1,512,1024]{2,3,1,0:T(8,128)(2,1)}, bf16[2,1,512,1024]{2,3,1,0:T(8,128)(2,1)}, u32[]{:S(2)}, u32[]{:S(2)}) %collective-permute-start.1) | collective-permute-done | bytes 2097184 | tf_op jit(solution)/shard_map/while/body/eval_jaxpr/ppermute | solution.py:16
  510.2 4.2 convert_element_type.563
  514.4 35.8 %collective-permute-done.2 = bf16[2,1,512,1024]{2,3,1,0:T(8,128)(2,1)} collective-permute-done((bf16[2,1,512,1024]{2,3,1,0:T(8,128)(2,1)S(1)}, bf16[2,1,512,1024]{2,3,1,0:T(8,128)(2,1)}, u32[]{:S(2)}, u32[]{:S(2)}) %collective-permute-start.2) | collective-permute-done | bytes 2097184 | tf_op jit(solution)/shard_map/while/body/eval_jaxpr/ppermute | solution.py:16
  552.7 3.3 copy.105
  558.5 3.9 convert_element_type.562
  562.4 3.5 collective-permute-start.1
  565.9 46.4 %collective-permute-done.1 = bf16[2,1,512,1024]{2,3,1,0:T(8,128)(2,1)} collective-permute-done((bf16[2,1,512,1024]{2,3,1,0:T(8,128)(2,1)}, bf16[2,1,512,1024]{2,3,1,0:T(8,128)(2,1)}, u32[]{:S(2)}, u32[]{:S(2)}) %collective-permute-start.1) | collective-permute-done | bytes 2097184 | tf_op jit(solution)/shard_map/while/body/eval_jaxpr/ppermute | solution.py:16
  612.3 4.2 convert_element_type.563
  616.5 34.9 %collective-permute-done.2 = bf16[2,1,512,1024]{2,3,1,0:T(8,128)(2,1)} collective-permute-done((bf16[2,1,512,1024]{2,3,1,0:T(8,128)(2,1)S(1)}, bf16[2,1,512,1024]{2,3,1,0:T(8,128)(2,1)}, u32[]{:S(2)}, u32[]{:S(2)}) %collective-permute-start.2) | collective-permute-done | bytes 2097184 | tf_op jit(solution)/shard_map/while/body/eval_jaxpr/ppermute | solution.py:16
  656.4 4.0 convert_element_type.365
  660.4 45.7 %collective-permute-start.3 = (bf16[2,1,512,1024]{2,3,1,0:T(8,128)(2,1)}, bf16[2,1,512,1024]{2,3,1,0:T(8,128)(2,1)}, u32[]{:S(2)}, u32[]{:S(2)}) collective-permute-start(bf16[2,1,512,1024]{2,3,1,0:T(8,128)(2,1)} %convert_element_type.365), channel_id=1, source_target_pairs={{0,3},{1,0},{2,1},{3,2},{4,7},{5,4},{6,5},{7,6},{8,11},{9,8},{10,9... | collective-permute-start | bytes 6291464 | tf_op jit(solution)/shard_map/ppermute | solution.py:16
  706.2 6.8 convolution_bitcast_fusion.1
  717.4 7.0 copy.65
  724.5 8.2 convolution_bitcast_fusion
  732.7 8.3 copy.66
  741.1 4.8 collective-permute-done.3
  774.4 880.8 %all-reduce.14 = (bf16[1048576]{0:T(1024)(128)(2,1)}, bf16[1048576]{0:T(1024)(128)(2,1)}, bf16[1048576]{0:T(1024)(128)(2,1)}, bf16[1048576]{0:T(1024)(128)(2,1)}...) all-reduce(f32[1048576]{0:T(1024)} %bitcast.346, ...), channel_id=2, replica_groups=mesh['dp'=8,'blk'=4] {'dp','blk'}, use_global_device_ids=true, to_apply=%region_43.44.clone | all-reduce | flops 12591104 | bytes 75546624
  1664.9 63.7 %all-gather.1 = bf16[32,1,128]{2,1,0:T(2,128)(2,1)S(1)} all-gather(bf16[1,1,128]{2,1,0:T(2,128)(2,1)S(1)} %fusion.122), channel_id=1, replica_groups=mesh['dp'=8,'blk'=4] {'dp','blk'}, dimensions={0}, use_global_device_ids=true | all-gather | bytes 8448 | tf_op jit(solution)/shard_map/all_gather | solution.py:304
  1728.7 64.5 %all-gather = bf16[32,1,128]{2,1,0:T(2,128)(2,1)S(1)} all-gather(bf16[1,1,128]{2,1,0:T(2,128)(2,1)S(1)} %fusion.123), channel_id=1, replica_groups=mesh['dp'=8,'blk'=4] {'dp','blk'}, dimensions={0}, use_global_device_ids=true | all-gather | bytes 8448 | tf_op jit(solution)/shard_map/all_gather | solution.py:295
  1794.5 4.0 fusion.96
  1798.5 4.5 reshape.1697
  1802.9 4.5 reshape.1699
  1807.4 20.4 all-gather.13.cloned.1.call-done
  1827.9 4.5 reshape.1701
  1832.3 53.5 %all-gather.15.cloned.1.call-done = bf16[1048576]{0:T(1024)(128)(2,1)} async-done(((bf16[32768]{0:T(1024)(128)(2,1)}), bf16[1048576]{0:T(1024)(128)(2,1)}) %all-gather.15.cloned.1.call-update) | async-done | bytes 2097168 | tf_op jit(solution)/shard_map/all_gather | solution.py:292
  1885.9 4.5 reshape.1703
  1890.3 75.3 %all-gather.17.cloned.1.call-done = bf16[4194304]{0:T(1024)(128)(2,1)} async-done(((bf16[131072]{0:T(1024)(128)(2,1)}), bf16[4194304]{0:T(1024)(128)(2,1)}) %all-gather.17.cloned.1.call-update) | async-done | bytes 8388624 | tf_op jit(solution)/shard_map/all_gather | solution.py:298
  1965.6 14.5 reshape.1705
  1980.1 64.4 %all-gather.19.cloned.1.call-done = bf16[4194304]{0:T(1024)(128)(2,1)} async-done(((bf16[131072]{0:T(1024)(128)(2,1)}), bf16[4194304]{0:T(1024)(128)(2,1)}) %all-gather.19.cloned.1.call-update) | async-done | bytes 8388624 | tf_op jit(solution)/shard_map/all_gather | solution.py:301
  2044.5 14.6 reshape.1707
  (307 shorter events, 133.5 us)
Async XLA Ops:
  7.2 211.3 %copy-start = (bf16[1024,1024]{1,0:T(8,128)(2,1)S(1)}, bf16[1024,1024]{1,0:T(8,128)(2,1)}, u32[]{:S(2)}) copy-start(bf16[1024,1024]{1,0:T(8,128)(2,1)} %param.29) | copy-start | bytes 6291460
  7.2 1791.3 %all-gather.9.cloned.1.call-start = ((), (), s32[]{:S(2)}) async-start(), calls=%async_computation | async-start | bytes 2162688 | tf_op jit(solution)/shard_map/all_gather | solution.py:283
  8.8 18.8 copy-start.63
  10.3 17.3 copy-start.39
  11.7 31.9 %copy-start.45 = (s32[512]{0:T(512)}, s32[512]{0:T(512)S(1)}, u32[]{:S(2)}) copy-start(s32[512]{0:T(512)S(1)} %get-tuple-element.1555) | copy-start | bytes 6148
  14.2 4.0 copy-start.6
  18.5 9.1 copy-start.42
  18.9 4.0 copy-start.49
  18.9 8.7 copy-start.47
  22.9 3.2 copy-start.29
  40.4 3.1 copy-start.30
  40.4 3.1 copy-start.31
  53.3 4.0 copy-start.17
  57.3 5.3 copy-start.18
  62.8 49.1 %collective-permute-start = (bf16[2,1,512,1024]{2,3,1,0:T(8,128)(2,1)}, bf16[2,1,512,1024]{2,3,1,0:T(8,128)(2,1)}, u32[]{:S(2)}, u32[]{:S(2)}) collective-permute-start(bf16[2,1,512,1024]{2,3,1,0:T(8,128)(2,1)} %get-tuple-element.1468), channel_id=1, source_target_pairs={{0,3},{1,0},{2,1},{3,2},{4,7},{5,4},{6,5},{7,6},{8,11},{9,8},{10,9... | collective-permute-start | bytes 6291464 | tf_op jit(solution)/shard_map/while/body/eval_jaxpr/ppermute | solution.py:16
  115.0 47.7 %collective-permute-start = (bf16[2,1,512,1024]{2,3,1,0:T(8,128)(2,1)}, bf16[2,1,512,1024]{2,3,1,0:T(8,128)(2,1)}, u32[]{:S(2)}, u32[]{:S(2)}) collective-permute-start(bf16[2,1,512,1024]{2,3,1,0:T(8,128)(2,1)} %get-tuple-element.1468), channel_id=1, source_target_pairs={{0,3},{1,0},{2,1},{3,2},{4,7},{5,4},{6,5},{7,6},{8,11},{9,8},{10,9... | collective-permute-start | bytes 6291464 | tf_op jit(solution)/shard_map/while/body/eval_jaxpr/ppermute | solution.py:16
  165.8 46.8 %collective-permute-start = (bf16[2,1,512,1024]{2,3,1,0:T(8,128)(2,1)}, bf16[2,1,512,1024]{2,3,1,0:T(8,128)(2,1)}, u32[]{:S(2)}, u32[]{:S(2)}) collective-permute-start(bf16[2,1,512,1024]{2,3,1,0:T(8,128)(2,1)} %get-tuple-element.1468), channel_id=1, source_target_pairs={{0,3},{1,0},{2,1},{3,2},{4,7},{5,4},{6,5},{7,6},{8,11},{9,8},{10,9... | collective-permute-start | bytes 6291464 | tf_op jit(solution)/shard_map/while/body/eval_jaxpr/ppermute | solution.py:16
  221.8 50.7 %copy-start.9 = (f32[512,1024]{1,0:T(8,128)}, f32[512,1024]{1,0:T(8,128)S(1)}, u32[]{:S(2)}) copy-start(f32[512,1024]{1,0:T(8,128)S(1)} %get-tuple-element.1230) | copy-start | bytes 6291460
  221.8 50.6 %copy-start.51 = (f32[512]{0:T(512)}, f32[512]{0:T(512)S(1)}, u32[]{:S(2)}) copy-start(f32[512]{0:T(512)S(1)} %broadcast_multiply_fusion.1) | copy-start | bytes 6148
  222.2 50.3 %copy-start.61 = (f32[512]{0:T(512)}, f32[512]{0:T(512)S(1)}, u32[]{:S(2)}) copy-start(f32[512]{0:T(512)S(1)} %fusion.120) | copy-start | bytes 6148
  230.5 3.4 copy-start.73
  243.0 2.3 copy-start.57
  247.5 15.6 copy-start.23
  247.5 15.6 copy-start.69
  276.3 3.6 copy-start.71
  286.1 368.0 %copy-start.46 = (s32[512]{0:T(512)S(1)}, s32[512]{0:T(512)}, u32[]{:S(2)}) copy-start(s32[512]{0:T(512)} %copy-done.45) | copy-start | bytes 6148
  288.8 3.3 copy-start.3
  336.2 24.5 %copy-start.2 = (bf16[2,1,512,1024]{2,3,1,0:T(8,128)(2,1)S(1)}, bf16[2,1,512,1024]{2,3,1,0:T(8,128)(2,1)}, u32[]{:S(2)}) copy-start(bf16[2,1,512,1024]{2,3,1,0:T(8,128)(2,1)} %copy.105) | copy-start | bytes 6291460 | tf_op jit(solution)/shard_map/while
  340.1 67.0 %collective-permute-start.1 = (bf16[2,1,512,1024]{2,3,1,0:T(8,128)(2,1)}, bf16[2,1,512,1024]{2,3,1,0:T(8,128)(2,1)}, u32[]{:S(2)}, u32[]{:S(2)}) collective-permute-start(bf16[2,1,512,1024]{2,3,1,0:T(8,128)(2,1)} %convert_element_type.562), channel_id=1, source_target_pairs={{0,3},{1,0},{2,1},{3,2},{4,7},{5,4},{6,5},{7,6},{8,11},{9,8},{10,9... | collective-permute-start | bytes 6291464 | tf_op jit(solution)/shard_map/while/body/eval_jaxpr/ppermute | solution.py:16
  360.7 87.3 %collective-permute-start.2 = (bf16[2,1,512,1024]{2,3,1,0:T(8,128)(2,1)S(1)}, bf16[2,1,512,1024]{2,3,1,0:T(8,128)(2,1)}, u32[]{:S(2)}, u32[]{:S(2)}) collective-permute-start(bf16[2,1,512,1024]{2,3,1,0:T(8,128)(2,1)S(1)} %copy-done.2), channel_id=1, source_target_pairs={{0,3},{1,0},{2,1},{3,2},{4,7},{5,4},{6,5},{7,6},{8,11},{9,8},{10,9... | collective-permute-start | bytes 6291464 | tf_op jit(solution)/shard_map/while/body/eval_jaxpr/ppermute | solution.py:16
  450.5 3.3 copy-start.3
  456.4 7.4 copy-start.2
  460.3 49.9 %collective-permute-start.1 = (bf16[2,1,512,1024]{2,3,1,0:T(8,128)(2,1)}, bf16[2,1,512,1024]{2,3,1,0:T(8,128)(2,1)}, u32[]{:S(2)}, u32[]{:S(2)}) collective-permute-start(bf16[2,1,512,1024]{2,3,1,0:T(8,128)(2,1)} %convert_element_type.562), channel_id=1, source_target_pairs={{0,3},{1,0},{2,1},{3,2},{4,7},{5,4},{6,5},{7,6},{8,11},{9,8},{10,9... | collective-permute-start | bytes 6291464 | tf_op jit(solution)/shard_map/while/body/eval_jaxpr/ppermute | solution.py:16
  463.8 86.4 %collective-permute-start.2 = (bf16[2,1,512,1024]{2,3,1,0:T(8,128)(2,1)S(1)}, bf16[2,1,512,1024]{2,3,1,0:T(8,128)(2,1)}, u32[]{:S(2)}, u32[]{:S(2)}) collective-permute-start(bf16[2,1,512,1024]{2,3,1,0:T(8,128)(2,1)S(1)} %copy-done.2), channel_id=1, source_target_pairs={{0,3},{1,0},{2,1},{3,2},{4,7},{5,4},{6,5},{7,6},{8,11},{9,8},{10,9... | collective-permute-start | bytes 6291464 | tf_op jit(solution)/shard_map/while/body/eval_jaxpr/ppermute | solution.py:16
  552.7 3.3 copy-start.3
  558.5 7.4 copy-start.2
  562.4 49.9 %collective-permute-start.1 = (bf16[2,1,512,1024]{2,3,1,0:T(8,128)(2,1)}, bf16[2,1,512,1024]{2,3,1,0:T(8,128)(2,1)}, u32[]{:S(2)}, u32[]{:S(2)}) collective-permute-start(bf16[2,1,512,1024]{2,3,1,0:T(8,128)(2,1)} %convert_element_type.562), channel_id=1, source_target_pairs={{0,3},{1,0},{2,1},{3,2},{4,7},{5,4},{6,5},{7,6},{8,11},{9,8},{10,9... | collective-permute-start | bytes 6291464 | tf_op jit(solution)/shard_map/while/body/eval_jaxpr/ppermute | solution.py:16
  565.9 85.5 %collective-permute-start.2 = (bf16[2,1,512,1024]{2,3,1,0:T(8,128)(2,1)S(1)}, bf16[2,1,512,1024]{2,3,1,0:T(8,128)(2,1)}, u32[]{:S(2)}, u32[]{:S(2)}) collective-permute-start(bf16[2,1,512,1024]{2,3,1,0:T(8,128)(2,1)S(1)} %copy-done.2), channel_id=1, source_target_pairs={{0,3},{1,0},{2,1},{3,2},{4,7},{5,4},{6,5},{7,6},{8,11},{9,8},{10,9... | collective-permute-start | bytes 6291464 | tf_op jit(solution)/shard_map/while/body/eval_jaxpr/ppermute | solution.py:16
  656.4 49.7 %copy-start.10 = (f32[512,1024]{1,0:T(8,128)S(1)}, f32[512,1024]{1,0:T(8,128)}, u32[]{:S(2)}) copy-start(f32[512,1024]{1,0:T(8,128)} %copy-done.9) | copy-start | bytes 6291460
  656.4 49.7 %copy-start.52 = (f32[512]{0:T(512)S(1)}, f32[512]{0:T(512)}, u32[]{:S(2)}) copy-start(f32[512]{0:T(512)} %copy-done.51) | copy-start | bytes 6148
  656.4 49.7 %copy-start.59 = (f32[1,1024]{1,0:T(1,128)S(1)}, f32[1,1024]{1,0:T(1,128)}, u32[]{:S(2)}) copy-start(f32[1,1024]{1,0:T(1,128)} %get-tuple-element.1271) | copy-start | bytes 12292
  656.4 49.7 %copy-start.62 = (f32[512]{0:T(512)S(1)}, f32[512]{0:T(512)}, u32[]{:S(2)}) copy-start(f32[512]{0:T(512)} %copy-done.61) | copy-start | bytes 6148
  656.4 49.7 %copy-start.66 = (f32[1,1024]{1,0:T(1,128)S(1)}, f32[1,1024]{1,0:T(1,128)}, u32[]{:S(2)}) copy-start(f32[1,1024]{1,0:T(1,128)} %get-tuple-element.1275) | copy-start | bytes 12292
  660.4 52.6 %copy-start.20 = (bf16[1,512,16,64]{1,3,2,0:T(8,128)(2,1)S(1)}, bf16[1,512,16,64]{1,3,2,0:T(8,128)(2,1)}, u32[]{:S(2)}) copy-start(bf16[1,512,16,64]{1,3,2,0:T(8,128)(2,1)} %copy-done.19) | copy-start | bytes 3145732
  660.4 52.6 %copy-start.28 = (f32[512,1024]{1,0:T(8,128)S(1)}, f32[512,1024]{1,0:T(8,128)}, u32[]{:S(2)}) copy-start(f32[512,1024]{1,0:T(8,128)} %copy-done.27) | copy-start | bytes 6291460
  660.4 52.6 %copy-start.72 = (f32[512]{0:T(512)S(1)}, f32[512]{0:T(512)}, u32[]{:S(2)}) copy-start(f32[512]{0:T(512)} %copy-done.71) | copy-start | bytes 6148
  660.4 85.5 %collective-permute-start.3 = (bf16[2,1,512,1024]{2,3,1,0:T(8,128)(2,1)}, bf16[2,1,512,1024]{2,3,1,0:T(8,128)(2,1)}, u32[]{:S(2)}, u32[]{:S(2)}) collective-permute-start(bf16[2,1,512,1024]{2,3,1,0:T(8,128)(2,1)} %convert_element_type.365), channel_id=1, source_target_pairs={{0,3},{1,0},{2,1},{3,2},{4,7},{5,4},{6,5},{7,6},{8,11},{9,8},{10,9... | collective-permute-start | bytes 6291464 | tf_op jit(solution)/shard_map/ppermute | solution.py:16
  717.4 7.1 copy-start.24
  717.4 7.1 copy-start.70
  732.7 8.3 copy-start.55
  732.7 8.3 copy-start.56
  732.7 8.3 copy-start.67
  732.7 8.3 copy-start.68
  741.1 6.3 copy-start.22
  741.1 6.3 copy-start.36
  741.1 6.3 copy-start.38
  758.4 2.9 copy-start.50
  761.3 12.1 copy-start.13
  1656.7 146.3 %all-gather.11.cloned.1.call-start = ((), (), s32[]{:S(2)}) async-start(), calls=%async_computation.1 | async-start | bytes 2162688 | tf_op jit(solution)/shard_map/all_gather | solution.py:286
  1658.2 169.6 %all-gather.13.cloned.1.call-start = ((), (), s32[]{:S(2)}) async-start(), calls=%async_computation.2 | async-start | bytes 2162688 | tf_op jit(solution)/shard_map/all_gather | solution.py:289
  1659.8 226.1 %all-gather.15.cloned.1.call-start = ((), (), s32[]{:S(2)}) async-start(), calls=%async_computation.3 | async-start | bytes 2162688 | tf_op jit(solution)/shard_map/all_gather | solution.py:292
  1661.3 304.2 %all-gather.17.cloned.1.call-start = ((), (), s32[]{:S(2)}) async-start(), calls=%async_computation.4 | async-start | bytes 8650752 | tf_op jit(solution)/shard_map/all_gather | solution.py:298
  1663.1 381.4 %all-gather.19.cloned.1.call-start = ((), (), s32[]{:S(2)}) async-start(), calls=%async_computation.5 | async-start | bytes 8650752 | tf_op jit(solution)/shard_map/all_gather | solution.py:301
  2044.5 14.6 copy-start.1
  (24 other events, 31.4 us)
Sparse Core Ops, SparseCore 0:
  1656.8 53.4 all-gather.8
  1713.8 55.2 all-gather.10
  1772.6 55.2 all-gather.12
  1830.6 55.2 all-gather.14
  1889.1 76.3 all-gather.16
  1968.3 76.1 all-gather.18
where the time goes:
time: 2050 us; the launch traced here: 2070 us
  blocking collectives  1010 us (49%)
  waiting for transfers between devices  590 us (29%)
  local copies, waits for them, and re-layouts  158 us (8%)
  matrix products  122 us (6%)
  starting transfers between devices  84.4 us (4%)
  other arithmetic  75.8 us (4%)
    unnamed x1, blocking collectives  881 us
    ppermute x10, waiting for transfers between devices, passed_along(): return lax.ppermute(value, axis, pairs)  377 us
    ppermute x10, starting transfers between devices, passed_along(): return lax.ppermute(value, axis, pairs)  84.1 us
    all_gather x1, waiting for transfers between devices, shards(): lax.all_gather(shares[5].astype(jnp.bfloat16), ('dp', 'blk'), axis=0, til...  75.3 us
    all_gather x1, blocking collectives, shards(): lax.all_gather(shares[4].astype(jnp.bfloat16), ('dp', 'blk'), axis=0, til...  64.5 us
    all_gather x1, waiting for transfers between devices, shards(): lax.all_gather(shares[6].astype(jnp.bfloat16), ('dp', 'blk'), axis=0, til...  64.4 us
    unnamed x146, local copies, waits for them, and re-layouts  64.2 us
    all_gather x1, blocking collectives, shards(): lax.all_gather(shares[7].astype(jnp.bfloat16), ('dp', 'blk'), axis=0, til...  63.7 us
  transfers between devices with their start and end apart: 16, of which 14 were waited for; matrix products, arithmetic and copies ran while one was open for 5% of the time, Pallas kernels for 0%

commit v1 on v0

--- a/solution.py
+++ b/solution.py
@@ -1,6 +1,8 @@
 import jax
 import jax.numpy as jnp
 from jax import lax
+from jax.experimental import pallas as pl
+from jax.experimental.pallas import tpu as pltpu
 from jax.sharding import PartitionSpec as P
 
 HEAD = 64
@@ -64,6 +66,187 @@
     return lax.dot_general(
         left, right, (((1,), (1,)), ((), ())), preferred_element_type=jnp.float32
     )
+
+
+def stage_partners(n_dp, n_blk):
+    dp, blk = lax.axis_index("dp"), lax.axis_index("blk")
+    core = dp % 2
+    stages = []
+
+    def flipped(value, stride):
+        bit = (value // stride) % 2
+        return value + stride * (1 - 2 * bit), bit
+
+    other, bit = flipped(dp, 1)
+    stages.append(((other, blk), bit))
+    blk_bits = n_blk.bit_length() - 1
+    for step in range(blk_bits):
+        stride = (1 - core) * (1 << step) + core * (1 << (blk_bits - 1 - step))
+        other, bit = flipped(blk, stride)
+        stages.append(((dp, other), bit))
+    for step in range(1, n_dp.bit_length() - 1):
+        other, bit = flipped(dp, 1 << step)
+        stages.append(((other, blk), bit))
+    return stages
+
+
+class Reducer:
+    def __init__(self, stages, jobs, sub, grads, out, acc, recvs, sems):
+        self.stages, self.jobs, self.sub = stages, jobs, sub
+        self.grads, self.out, self.acc, self.recvs = grads, out, acc, recvs
+        self.own_sem, self.place_sem, self.send_sems, self.recv_sems = sems
+        self.count = len(stages)
+        self.held = [(0, sub)]
+        for _, bit in stages:
+            low, size = self.held[-1]
+            self.held.append((low + bit * (size // 2), size // 2))
+        self.ticks = jobs + 2 * self.count
+
+    @staticmethod
+    def scratch(count, jobs, sub, width):
+        return [
+            pltpu.VMEM((jobs, sub // 2, width), jnp.bfloat16),
+            [pltpu.VMEM((jobs, sub >> (k + 1), width), jnp.bfloat16) for k in range(count)],
+            (
+                pltpu.SemaphoreType.DMA,
+                pltpu.SemaphoreType.DMA,
+                pltpu.SemaphoreType.DMA((2 * count,)),
+                pltpu.SemaphoreType.DMA((2 * count, jobs)),
+            ),
+        ]
+
+    def rows(self, start, size):
+        return pl.ds(pl.multiple_of(start, 16), size)
+
+    def scatter_copy(self, k, j):
+        partner, bit = self.stages[k]
+        low, size = self.held[k]
+        half = size // 2
+        sent = low + (1 - bit) * half
+        if k == 0:
+            src = self.grads.at[self.rows(j * self.sub + sent, half)]
+        else:
+            src = self.acc.at[j, self.rows(sent - self.held[1][0], half)]
+        return pltpu.make_async_remote_copy(
+            src_ref=src,
+            dst_ref=self.recvs[k].at[j],
+            send_sem=self.send_sems.at[k],
+            recv_sem=self.recv_sems.at[k, j],
+            device_id=partner,
+            device_id_type=pl.DeviceIdType.MESH,
+        )
+
+    def gather_copy(self, k, j):
+        partner, _ = self.stages[k]
+        low, size = self.held[k + 1]
+        there = self.out.at[self.rows(j * self.sub + low, size)]
+        here = there
+        if k == self.count - 1:
+            here = self.acc.at[j, self.rows(low - self.held[1][0], size)]
+        return pltpu.make_async_remote_copy(
+            src_ref=here,
+            dst_ref=there,
+            send_sem=self.send_sems.at[self.count + k],
+            recv_sem=self.recv_sems.at[self.count + k, j],
+            device_id=partner,
+            device_id_type=pl.DeviceIdType.MESH,
+        )
+
+    def own_copy(self, j):
+        low, size = self.held[1]
+        return pltpu.make_async_copy(
+            self.grads.at[self.rows(j * self.sub + low, size)], self.acc.at[j], self.own_sem
+        )
+
+    def place_copy(self, j):
+        low, size = self.held[-1]
+        return pltpu.make_async_copy(
+            self.acc.at[j, self.rows(low - self.held[1][0], size)],
+            self.out.at[self.rows(j * self.sub + low, size)],
+            self.place_sem,
+        )
+
+    def launch(self, copy_of, k, j):
+        @pl.when(j >= 1)
+        def _():
+            copy_of(k, j - 1).wait_send()
+
+        copy_of(k, j).start()
+
+    def step(self, s, j):
+        count = self.count
+        if s == 0:
+            self.own_copy(j).start()
+            self.launch(self.scatter_copy, 0, j)
+        elif s <= count:
+            k = s - 1
+            self.scatter_copy(k, j).wait_recv()
+            if k == 0:
+                self.own_copy(j).wait()
+            low, size = self.held[k + 1]
+            mine = self.rows(low - self.held[1][0], size)
+            total = self.acc[j, mine].astype(jnp.float32) + self.recvs[k][j].astype(jnp.float32)
+            self.acc[j, mine] = total.astype(jnp.bfloat16)
+            if s < count:
+                self.launch(self.scatter_copy, s, j)
+            else:
+                self.place_copy(j).start()
+                self.launch(self.gather_copy, count - 1, j)
+        else:
+            k = 2 * count - s
+            self.gather_copy(k, j).wait_recv()
+            if s == count + 1:
+                self.place_copy(j).wait()
+            if k > 0:
+                self.launch(self.gather_copy, k - 1, j)
+
+    def tick(self, t):
+        for s in reversed(range(2 * self.count + 1)):
+            j = t - s
+
+            @pl.when((j >= 0) & (j < self.jobs))
+            def _(s=s, j=j):
+                self.step(s, j)
+
+    def finish(self):
+        for k in range(self.count):
+            self.scatter_copy(k, self.jobs - 1).wait_send()
+            self.gather_copy(k, self.jobs - 1).wait_send()
+
+
+def greet(partners):
+    barrier = pltpu.get_barrier_semaphore()
+    for partner in partners:
+        pl.semaphore_signal(
+            barrier, inc=1, device_id=partner, device_id_type=pl.DeviceIdType.MESH
+        )
+    pl.semaphore_wait(barrier, len(partners))
+
+
+def reduce_all(grads, n_dp, n_blk):
+    total, width = grads.shape
+    devices = n_dp * n_blk
+    sub = max(512, 16 * devices)
+    jobs = total // sub
+    count = devices.bit_length() - 1
+
+    def kernel(grads_ref, out_ref, acc, recvs, sems):
+        stages = stage_partners(n_dp, n_blk)
+        greet([partner for partner, _ in stages])
+        reducer = Reducer(stages, jobs, sub, grads_ref, out_ref, acc, recvs, sems)
+        lax.fori_loop(0, reducer.ticks, lambda t, c: (reducer.tick(t), c)[1], 0)
+        reducer.finish()
+
+    return pl.pallas_call(
+        kernel,
+        out_shape=jax.ShapeDtypeStruct((total, width), jnp.bfloat16),
+        in_specs=[pl.BlockSpec(memory_space=pl.ANY)],
+        out_specs=pl.BlockSpec(memory_space=pl.ANY),
+        scratch_shapes=Reducer.scratch(count, jobs, sub, width),
+        compiler_params=pltpu.CompilerParams(
+            collective_id=1, has_side_effects=True, vmem_limit_bytes=60 * 1024 * 1024
+        ),
+    )(grads)
 
 
 def shards(
@@ -257,68 +440,40 @@
     input_grad, gain_first, bias_first = first_back(normed_grad)
     grad_tokens = (hidden_grad + input_grad).astype(jnp.bfloat16).reshape(tokens.shape)
     early_norms = jnp.concatenate([gain_first, gain_second, bias_first, bias_second])
-    shares = (
-        lax.psum_scatter(
-            grad_query_weight.reshape(-1), ("dp", "blk"), scatter_dimension=0, tiled=True
-        ),
-        lax.psum_scatter(
-            grad_key_weight.reshape(-1), ("dp", "blk"), scatter_dimension=0, tiled=True
-        ),
-        lax.psum_scatter(
-            grad_value_weight.reshape(-1), ("dp", "blk"), scatter_dimension=0, tiled=True
-        ),
-        lax.psum_scatter(
-            grad_out_weight.reshape(-1), ("dp", "blk"), scatter_dimension=0, tiled=True
-        ),
-        lax.psum_scatter(early_norms, ("dp", "blk"), scatter_dimension=0, tiled=True),
-        lax.psum_scatter(
-            grad_up_weight.reshape(-1), ("dp", "blk"), scatter_dimension=0, tiled=True
-        ),
-        lax.psum_scatter(
-            grad_down_weight.reshape(-1), ("dp", "blk"), scatter_dimension=0, tiled=True
-        ),
-        lax.psum_scatter(late_norms, ("dp", "blk"), scatter_dimension=0, tiled=True),
-    )
-    summed = (
-        lax.all_gather(shares[0].astype(jnp.bfloat16), ("dp", "blk"), axis=0, tiled=True).astype(
-            jnp.float32
-        ),
-        lax.all_gather(shares[1].astype(jnp.bfloat16), ("dp", "blk"), axis=0, tiled=True).astype(
-            jnp.float32
-        ),
-        lax.all_gather(shares[2].astype(jnp.bfloat16), ("dp", "blk"), axis=0, tiled=True).astype(
-            jnp.float32
-        ),
-        lax.all_gather(shares[3].astype(jnp.bfloat16), ("dp", "blk"), axis=0, tiled=True).astype(
-            jnp.float32
-        ),
-        lax.all_gather(shares[4].astype(jnp.bfloat16), ("dp", "blk"), axis=0, tiled=True).astype(
-            jnp.float32
-        ),
-        lax.all_gather(shares[5].astype(jnp.bfloat16), ("dp", "blk"), axis=0, tiled=True).astype(
-            jnp.float32
-        ),
-        lax.all_gather(shares[6].astype(jnp.bfloat16), ("dp", "blk"), axis=0, tiled=True).astype(
-            jnp.float32
-        ),
-        lax.all_gather(shares[7].astype(jnp.bfloat16), ("dp", "blk"), axis=0, tiled=True).astype(
-            jnp.float32
-        ),
-    )
-    square_shape = (model_width, model_width)
-    norm_early = summed[4].reshape(4, model_width)
-    norm_late = summed[7].reshape(4, model_width)
+    low_grads = [
+        value.astype(jnp.bfloat16).reshape(-1, model_width)
+        for value in (
+            grad_down_weight,
+            jnp.swapaxes(grad_up_weight.reshape(model_width, -1, model_width), 0, 1),
+            grad_out_weight,
+            grad_query_weight,
+            grad_key_weight,
+            grad_value_weight,
+        )
+    ]
+    stacked = jnp.concatenate(low_grads)
+    summed_rows = reduce_all(stacked, lax.axis_size("dp"), lax.axis_size("blk"))
+    norms = lax.psum(jnp.concatenate([early_norms, late_norms]), ("dp", "blk"))
+    norm_early = norms[: 4 * model_width].reshape(4, model_width)
+    norm_late = norms[4 * model_width :].reshape(4, model_width)
+    ff = grad_down_weight.shape[0]
+    summed_rows = summed_rows.astype(jnp.float32)
+    squares = summed_rows[2 * ff :].reshape(4, model_width, model_width)
+    grad_down = summed_rows[:ff]
+    grad_up = jnp.swapaxes(
+        summed_rows[ff : 2 * ff].reshape(-1, model_width, model_width), 0, 1
+    ).reshape(model_width, ff)
     grad_gain = jnp.stack([norm_early[0], norm_early[1], norm_late[0], norm_late[1]])
     grad_bias = jnp.stack([norm_early[2], norm_early[3], norm_late[2], norm_late[3]])
     return (
         mixed,
         grad_tokens,
-        summed[0].reshape(square_shape),
-        summed[1].reshape(square_shape),
-        summed[2].reshape(square_shape),
-        summed[3].reshape(square_shape),
-        summed[5].reshape(model_width, -1),
-        summed[6].reshape(-1, model_width),
+        squares[1],
+        squares[2],
+        squares[3],
+        squares[0],
+        grad_up,
+        grad_down,
         grad_gain,
         grad_bias,
     )

time: 2050 us -> 1110 us (0.54); the launches traced: 2070 us -> 1100 us
  blocking collectives: 1010 us -> 44.2 us
  Pallas kernels: 0 us -> 248 us
  waiting for transfers between devices: 590 us -> 374 us
  local copies, waits for them, and re-layouts: 158 us -> 128 us
    unnamed x1 -> x0, blocking collectives: 881 us -> none
    pallas_call x0 -> x1, Pallas kernels: none -> 248 us  [reduce_all(): pl.pallas_call(kernel, out_shape=jax.ShapeDtypeStruct((total, width), jnp...]
    all_gather x6 -> x0, waiting for transfers between devices: 214 us -> none  [the longest x1 75.3 us: shards(): lax.all_gather(shares[5].astype(jnp.bfloat16), ('dp', 'blk'), axis=0, til...]
    all_gather x2 -> x0, blocking collectives: 128 us -> none  [the longest x1 64.5 us: shards(): lax.all_gather(shares[4].astype(jnp.bfloat16), ('dp', 'blk'), axis=0, til...]
    psum x0 -> x1, blocking collectives: none -> 44.2 us  [shards(): norms = lax.psum(jnp.concatenate([early_norms, late_norms]), ('dp', 'blk'))]
    reshape x6 -> x1, local copies, waits for them, and re-layouts: 47 us -> 12 us  [shards(): grad_up = jnp.swapaxes(summed_rows[ff:2 * ff].reshape(-1, model_width, mo...]
    unnamed x146 -> x156, local copies, waits for them, and re-layouts: 64.2 us -> 30.3 us
    slice x1 -> x2, local copies, waits for them, and re-layouts: 0.01 us -> 28.6 us  [the longest x1 18.4 us: shards(): grad_down = summed_rows[:ff]]
  transfers between devices with their start and end apart: 16 -> 10, of which waited for: 14 -> 10; matrix products, arithmetic and copies ran while one was open for 5% -> 5% of each run, Pallas kernels for 0% -> 0%
where the time goes in v1:
time: 1110 us; the launch traced here: 1100 us
  waiting for transfers between devices  374 us (34%)
  Pallas kernels  248 us (22%)
  local copies, waits for them, and re-layouts  128 us (12%)
  matrix products  126 us (11%)
  other arithmetic  82.8 us (7%)
  starting transfers between devices  82.8 us (7%)
  blocking collectives  44.2 us (4%)
    ppermute x10, waiting for transfers between devices, passed_along(): return lax.ppermute(value, axis, pairs)  374 us
    pallas_call x1, Pallas kernels, reduce_all(): pl.pallas_call(kernel, out_shape=jax.ShapeDtypeStruct((total, width), jnp...  248 us
    ppermute x10, starting transfers between devices, passed_along(): return lax.ppermute(value, axis, pairs)  82.8 us
    psum x1, blocking collectives, shards(): norms = lax.psum(jnp.concatenate([early_norms, late_norms]), ('dp', 'blk'))  44.2 us
    dot_general x6, matrix products, contract_cols(): lax.dot_general(left, right, (((1,), (1,)), ((), ())), preferred_element_...  32.2 us
    dot_general x6, matrix products, contract_rows(): lax.dot_general(left, right, (((0,), (0,)), ((), ())), preferred_element_...  30.4 us
    unnamed x156, local copies, waits for them, and re-layouts  30.3 us
    dot_general x6, matrix products, product(): return jnp.dot(left, right, preferred_element_type=jnp.float32)  28.8 us
  transfers between devices with their start and end apart: 10, of which 10 were waited for; matrix products, arithmetic and copies ran while one was open for 5% of the time, Pallas kernels for 0%

profile of v1, /device:TPU:0, one launch (start us, length us, event | category | flops | bytes accessed | tf_op | source)
XLA Modules:
  0.0 1099.1 jit_solution(12346292058528687558)
XLA Ops:
  10.5 4.0 copy.47
  19.6 3.9 copy.48
  23.6 3.2 fusion.100
  30.2 3.1 maximum_bitcast_fusion
  33.2 4.0 copy.51
  37.2 3.1 copy.82
  40.5 20.9 %conditional.4 = (f32[1,16,512]{2,1,0:T(8,128)}, f32[1,16,512]{2,1,0:T(8,128)S(1)}, f32[1,512,16,64]{1,3,2,0:T(8,128)}) conditional(s32[]{:T(128)} %bitcast.68, () %tuple.106, (s32[]{:T(128)}, s32[512]{0:T(512)S(1)}, s32[512]{0:T(512)S(1)}, s32[1,16]{1,0:T(1,128)S(1)}, s32[1,512]{1,0:T(1,128)S(1)}, /*index=5*/bf16[1,512,16,64]{1,3,2,0:T(8,128)(2,1)S(1)}, ...), branch_computations={%region_5.6_spmd, %region_6.0_spmd} | conditional | flops 1129644032 | bytes 65454184 | solution.py:315
  40.8 3.9 copy.50
  46.8 3.4 fusion.8
  50.2 4.0 fusion.10
  54.8 5.2 bitcast_add_fusion
  61.3 152.8 %while.44 = (s32[]{:T(128)}, f32[1,16,512]{2,1,0:T(8,128)}, f32[1,16,512]{2,1,0:T(8,128)S(1)}, f32[1,512,16,64]{1,3,2,0:T(8,128)}, bf16[2,1,512,1024]{2,3,1,0:T(...) while((s32[]{:T(128)}, f32[1,16,512]{2,1,0:T(8,128)}, ...), condition=%wide.region_17.18_spmd.clone.clone, body=%wide.region_10.17_spmd.clone.clone.sunk | while | flops 1130177024 | bytes 76051080 | solution.py:329
  61.4 4.0 collective-permute-start
  67.8 42.7 %collective-permute-done = bf16[2,1,512,1024]{2,3,1,0:T(8,128)(2,1)} collective-permute-done((bf16[2,1,512,1024]{2,3,1,0:T(8,128)(2,1)}, bf16[2,1,512,1024]{2,3,1,0:T(8,128)(2,1)}, u32[]{:S(2)}, u32[]{:S(2)}) %collective-permute-start) | collective-permute-done | bytes 2097184 | tf_op jit(solution)/shard_map/while/body/eval_jaxpr/ppermute | solution.py:18
  110.5 3.0 copy.92
  113.6 3.4 collective-permute-start
  119.4 41.8 %collective-permute-done = bf16[2,1,512,1024]{2,3,1,0:T(8,128)(2,1)} collective-permute-done((bf16[2,1,512,1024]{2,3,1,0:T(8,128)(2,1)}, bf16[2,1,512,1024]{2,3,1,0:T(8,128)(2,1)}, u32[]{:S(2)}, u32[]{:S(2)}) %collective-permute-start) | collective-permute-done | bytes 2097184 | tf_op jit(solution)/shard_map/while/body/eval_jaxpr/ppermute | solution.py:18
  161.3 3.0 copy.92
  164.3 3.4 collective-permute-start
  170.2 40.9 %collective-permute-done = bf16[2,1,512,1024]{2,3,1,0:T(8,128)(2,1)} collective-permute-done((bf16[2,1,512,1024]{2,3,1,0:T(8,128)(2,1)}, bf16[2,1,512,1024]{2,3,1,0:T(8,128)(2,1)}, u32[]{:S(2)}, u32[]{:S(2)}) %collective-permute-start) | collective-permute-done | bytes 2097184 | tf_op jit(solution)/shard_map/while/body/eval_jaxpr/ppermute | solution.py:18
  211.1 3.0 copy.92
  221.0 7.4 fusion.124
  228.4 11.8 %fusion.150 = (f32[512]{0:T(512)S(1)}, f32[512,1024]{1,0:T(8,128)S(1)}) fusion(bf16[4096,1024]{1,0:T(8,128)(2,1)} %param.31, f32[512,4096]{1,0:T(8,128)S(1)} %fusion.124), kind=kOutput, calls=%fused_computation.255 | convolution fusion | flops 4314365440 | bytes 18876416 | tf_op jit(solution)/shard_map/dot_general | solution.py:56
  245.1 13.2 %fusion.68 = bf16[512,4096]{1,0:T(8,128)(2,1)S(1)} fusion(f32[512,4096]{1,0:T(8,128)} %copy-done.77, bf16[4096,1024]{1,0:T(8,128)(2,1)} %param.31, f32[512,1024]{1,0:T(8,128)S(1)} %get-tuple-element.1192, f32[512]{0:T(512)S(1)} %negate_multiply_fusion.4), kind=kOutput, calls=%fused_computation.99 | convolution fusion | flops 4337958912 | bytes 23070720 | tf_op jit(solution)/shard_map/dot_general | solution.py:66
  258.4 9.7 multiply_reduce_fusion
  281.7 368.3 %while.45 = (s32[]{:T(128)}, f32[1,512,16,64]{1,3,2,0:T(8,128)}, f32[2,1,512,1024]{2,3,1,0:T(8,128)}, bf16[2,1,512,1024]{2,3,1,0:T(8,128)(2,1)}, s32[]{:T(128)},...) while((s32[]{:T(128)}, f32[1,512,16,64]{1,3,2,0:T(8,128)}, ...), condition=%wide.region_37.38_spmd.clone.clone, body=%wide.region_32.37_spmd.clone.clone.sunk | while | flops 2742338048 | bytes 222163696 | solution.py:422
  284.6 3.0 copy.100
  290.2 39.8 %conditional.13 = ((f32[1,512,16,64]{1,3,2,0:T(8,128)}, f32[2,1,512,1024]{2,3,1,0:T(8,128)})) conditional(s32[]{:T(128)} %convert_element_type.543, (f32[1,512,16,64]{1,3,2,0:T(8,128)}, f32[2,1,512,1024]{2,3,1,0:T(8,128)}) %tuple.235, (s32[]{:T(128)}, s32[512]{0:T(512)S(1)}, s32[]{:T(128)}, s32[1,16]{1,0:T(1,128)S(1)}, s32[1,512]{1,0:T(1,128)S(1)}, ...), branch_computations={%region_34.34_spmd, %region_35.36_spmd} | conditional | flops 2739167744 | bytes 180211872 | solution.py:406
  294.7 6.2 copy-done.1
  300.8 6.0 fusion.38
  306.9 10.3 multiply_convert_fusion
  318.6 5.5 bitcast_add_fusion.4
  324.1 5.9 maximum_add_fusion
  330.0 3.8 convert_element_type.544
  333.8 21.8 %collective-permute-start.1 = (bf16[2,1,512,1024]{2,3,1,0:T(8,128)(2,1)}, bf16[2,1,512,1024]{2,3,1,0:T(8,128)(2,1)}, u32[]{:S(2)}, u32[]{:S(2)}) collective-permute-start(bf16[2,1,512,1024]{2,3,1,0:T(8,128)(2,1)} %convert_element_type.544), channel_id=1, source_target_pairs={{0,3},{1,0},{2,1},{3,2},{4,7},{5,4},{6,5},{7,6},{8,11},{9,8},{10,9... | collective-permute-start | bytes 6291464 | tf_op jit(solution)/shard_map/while/body/eval_jaxpr/ppermute | solution.py:18
  355.6 46.4 %collective-permute-done.1 = bf16[2,1,512,1024]{2,3,1,0:T(8,128)(2,1)} collective-permute-done((bf16[2,1,512,1024]{2,3,1,0:T(8,128)(2,1)}, bf16[2,1,512,1024]{2,3,1,0:T(8,128)(2,1)}, u32[]{:S(2)}, u32[]{:S(2)}) %collective-permute-start.1) | collective-permute-done | bytes 2097184 | tf_op jit(solution)/shard_map/while/body/eval_jaxpr/ppermute | solution.py:18
  402.0 4.2 convert_element_type.545
  406.2 36.8 %collective-permute-done.2 = bf16[2,1,512,1024]{2,3,1,0:T(8,128)(2,1)} collective-permute-done((bf16[2,1,512,1024]{2,3,1,0:T(8,128)(2,1)}, bf16[2,1,512,1024]{2,3,1,0:T(8,128)(2,1)}, u32[]{:S(2)}, u32[]{:S(2)}) %collective-permute-start.2) | collective-permute-done | bytes 2097184 | tf_op jit(solution)/shard_map/while/body/eval_jaxpr/ppermute | solution.py:18
  445.5 3.0 copy.100
  448.6 4.7 broadcast_select_fusion.2
  453.2 3.8 convert_element_type.544
  457.0 3.4 collective-permute-start.1
  460.4 46.4 %collective-permute-done.1 = bf16[2,1,512,1024]{2,3,1,0:T(8,128)(2,1)} collective-permute-done((bf16[2,1,512,1024]{2,3,1,0:T(8,128)(2,1)}, bf16[2,1,512,1024]{2,3,1,0:T(8,128)(2,1)}, u32[]{:S(2)}, u32[]{:S(2)}) %collective-permute-start.1) | collective-permute-done | bytes 2097184 | tf_op jit(solution)/shard_map/while/body/eval_jaxpr/ppermute | solution.py:18
  506.8 4.2 convert_element_type.545
  511.0 35.9 %collective-permute-done.2 = bf16[2,1,512,1024]{2,3,1,0:T(8,128)(2,1)} collective-permute-done((bf16[2,1,512,1024]{2,3,1,0:T(8,128)(2,1)}, bf16[2,1,512,1024]{2,3,1,0:T(8,128)(2,1)}, u32[]{:S(2)}, u32[]{:S(2)}) %collective-permute-start.2) | collective-permute-done | bytes 2097184 | tf_op jit(solution)/shard_map/while/body/eval_jaxpr/ppermute | solution.py:18
  549.4 3.0 copy.100
  552.5 4.7 broadcast_select_fusion.2
  557.1 3.8 convert_element_type.544
  560.9 3.4 collective-permute-start.1
  564.3 46.4 %collective-permute-done.1 = bf16[2,1,512,1024]{2,3,1,0:T(8,128)(2,1)} collective-permute-done((bf16[2,1,512,1024]{2,3,1,0:T(8,128)(2,1)}, bf16[2,1,512,1024]{2,3,1,0:T(8,128)(2,1)}, u32[]{:S(2)}, u32[]{:S(2)}) %collective-permute-start.1) | collective-permute-done | bytes 2097184 | tf_op jit(solution)/shard_map/while/body/eval_jaxpr/ppermute | solution.py:18
  610.7 4.2 convert_element_type.545
  614.9 35.0 %collective-permute-done.2 = bf16[2,1,512,1024]{2,3,1,0:T(8,128)(2,1)} collective-permute-done((bf16[2,1,512,1024]{2,3,1,0:T(8,128)(2,1)}, bf16[2,1,512,1024]{2,3,1,0:T(8,128)(2,1)}, u32[]{:S(2)}, u32[]{:S(2)}) %collective-permute-start.2) | collective-permute-done | bytes 2097184 | tf_op jit(solution)/shard_map/while/body/eval_jaxpr/ppermute | solution.py:18
  654.0 4.2 convert_element_type.356
  658.2 43.4 %collective-permute-start.3 = (bf16[2,1,512,1024]{2,3,1,0:T(8,128)(2,1)}, bf16[2,1,512,1024]{2,3,1,0:T(8,128)(2,1)S(1)}, u32[]{:S(2)}, u32[]{:S(2)}) collective-permute-start(bf16[2,1,512,1024]{2,3,1,0:T(8,128)(2,1)} %convert_element_type.356), channel_id=1, source_target_pairs={{0,3},{1,0},{2,1},{3,2},{4,7},{5,4},{6,5},{7,6},{8,11},{9,8},{10,9... | collective-permute-start | bytes 6291464 | tf_op jit(solution)/shard_map/ppermute | solution.py:18
  701.7 10.2 convert_dynamic-update-slice_fusion
  711.9 7.3 convolution_convert_fusion
  719.3 8.1 copy.61
  727.4 7.7 constant_dynamic-update-slice_fusion
  735.1 4.3 convert_dynamic-update-slice_fusion.4
  759.7 247.9 %shard_map.186 = bf16[12288,1024]{1,0:T(8,128)(2,1)} custom-call(bf16[12288,1024]{1,0:T(8,128)(2,1)} %convert_dynamic-update-slice_fusion.1.grads_ref), custom_call_target="tpu_custom_call" | custom-call | tf_op jit(solution)/shard_map/pallas_call | solution.py:240
  1007.6 10.2 fusion.144
  1017.7 18.4 %fusion.143 = (f32[4096,1024]{1,0:T(8,128)}, f32[4096,1024]{1,0:T(8,128)}) fusion(bf16[12288,1024]{1,0:T(8,128)(2,1)} %shard_map.186), kind=kLoop, calls=%fused_computation.248 | loop fusion | bytes 67108864 | tf_op jit(solution)/shard_map/slice | solution.py:462
  1041.5 44.2 %psum.7 = f32[8192]{0:T(1024)S(1)} all-reduce(f32[8192]{0:T(1024)S(1)} %constant_dynamic-update-slice_fusion.3), channel_id=1, replica_groups=mesh['dp'=8,'blk'=4] {'dp','blk'}, use_global_device_ids=true, to_apply=%region_51.52 | all-reduce | flops 8192 | bytes 65536 | tf_op jit(solution)/shard_map/psum | solution.py:456
  1085.7 12.0 %copy.59 = f32[4,128,8,1024]{3,2,0,1:T(8,128)} copy(f32[4,128,8,1024]{3,2,1,0:T(8,128)} %bitcast.324) | data formatting | bytes 33554432 | tf_op jit(solution)/shard_map/reshape | solution.py:465
  (280 shorter events, 91.9 us)
Async XLA Ops:
  0.6 13.9 %copy-start = (bf16[1024,1024]{1,0:T(8,128)(2,1)S(1)}, bf16[1024,1024]{1,0:T(8,128)(2,1)}, u32[]{:S(2)}) copy-start(bf16[1024,1024]{1,0:T(8,128)(2,1)} %param.28) | copy-start | bytes 6291460
  0.7 8.6 copy-start.60
  0.7 9.2 copy-start.61
  3.7 19.8 %copy-start.43 = (f32[512]{0:T(512)}, f32[512]{0:T(512)S(1)}, u32[]{:S(2)}) copy-start(f32[512]{0:T(512)S(1)} %broadcast_multiply_fusion.3) | copy-start | bytes 6148
  5.4 9.2 copy-start.51
  5.4 18.1 %copy-start.49 = (f32[512]{0:T(512)}, f32[512]{0:T(512)S(1)}, u32[]{:S(2)}) copy-start(f32[512]{0:T(512)S(1)} %fusion.118) | copy-start | bytes 6148
  6.6 33.8 %copy-start.46 = (s32[512]{0:T(512)}, s32[512]{0:T(512)S(1)}, u32[]{:S(2)}) copy-start(s32[512]{0:T(512)S(1)} %get-tuple-element.1524) | copy-start | bytes 6148
  9.9 13.6 %copy-start.40 = (f32[1,1024]{1,0:T(1,128)}, f32[1,1024]{1,0:T(1,128)S(1)}, u32[]{:S(2)}) copy-start(f32[1,1024]{1,0:T(1,128)S(1)} %get-tuple-element.1240) | copy-start | bytes 12292
  10.5 13.0 %copy-start.69 = (f32[1,1024]{1,0:T(1,128)}, f32[1,1024]{1,0:T(1,128)S(1)}, u32[]{:S(2)}) copy-start(f32[1,1024]{1,0:T(1,128)S(1)} %get-tuple-element.1244) | copy-start | bytes 12292
  10.5 4.0 copy-start.5
  14.5 2.3 copy-start.30
  23.6 3.5 copy-start.26
  37.2 3.1 copy-start.31
  37.2 3.1 copy-start.32
  61.4 49.2 %collective-permute-start = (bf16[2,1,512,1024]{2,3,1,0:T(8,128)(2,1)}, bf16[2,1,512,1024]{2,3,1,0:T(8,128)(2,1)}, u32[]{:S(2)}, u32[]{:S(2)}) collective-permute-start(bf16[2,1,512,1024]{2,3,1,0:T(8,128)(2,1)} %get-tuple-element.1437), channel_id=1, source_target_pairs={{0,3},{1,0},{2,1},{3,2},{4,7},{5,4},{6,5},{7,6},{8,11},{9,8},{10,9... | collective-permute-start | bytes 6291464 | tf_op jit(solution)/shard_map/while/body/eval_jaxpr/ppermute | solution.py:18
  113.6 47.7 %collective-permute-start = (bf16[2,1,512,1024]{2,3,1,0:T(8,128)(2,1)}, bf16[2,1,512,1024]{2,3,1,0:T(8,128)(2,1)}, u32[]{:S(2)}, u32[]{:S(2)}) collective-permute-start(bf16[2,1,512,1024]{2,3,1,0:T(8,128)(2,1)} %get-tuple-element.1437), channel_id=1, source_target_pairs={{0,3},{1,0},{2,1},{3,2},{4,7},{5,4},{6,5},{7,6},{8,11},{9,8},{10,9... | collective-permute-start | bytes 6291464 | tf_op jit(solution)/shard_map/while/body/eval_jaxpr/ppermute | solution.py:18
  164.3 46.8 %collective-permute-start = (bf16[2,1,512,1024]{2,3,1,0:T(8,128)(2,1)}, bf16[2,1,512,1024]{2,3,1,0:T(8,128)(2,1)}, u32[]{:S(2)}, u32[]{:S(2)}) collective-permute-start(bf16[2,1,512,1024]{2,3,1,0:T(8,128)(2,1)} %get-tuple-element.1437), channel_id=1, source_target_pairs={{0,3},{1,0},{2,1},{3,2},{4,7},{5,4},{6,5},{7,6},{8,11},{9,8},{10,9... | collective-permute-start | bytes 6291464 | tf_op jit(solution)/shard_map/while/body/eval_jaxpr/ppermute | solution.py:18
  214.2 2.8 copy-start.23
  220.3 47.7 %copy-start.8 = (f32[512,1024]{1,0:T(8,128)}, f32[512,1024]{1,0:T(8,128)S(1)}, u32[]{:S(2)}) copy-start(f32[512,1024]{1,0:T(8,128)S(1)} %get-tuple-element.1194) | copy-start | bytes 6291460
  220.4 47.7 %copy-start.53 = (f32[512]{0:T(512)}, f32[512]{0:T(512)S(1)}, u32[]{:S(2)}) copy-start(f32[512]{0:T(512)S(1)} %broadcast_multiply_fusion.1) | copy-start | bytes 6148
  220.7 47.4 %copy-start.65 = (f32[512]{0:T(512)}, f32[512]{0:T(512)S(1)}, u32[]{:S(2)}) copy-start(f32[512]{0:T(512)S(1)} %fusion.120) | copy-start | bytes 6148
  228.4 11.8 %copy-start.77 = (f32[512,4096]{1,0:T(8,128)}, f32[512,4096]{1,0:T(8,128)S(1)}, u32[]{:S(2)}) copy-start(f32[512,4096]{1,0:T(8,128)S(1)} %fusion.124) | copy-start | bytes 25165828
  240.6 2.3 copy-start.59
  245.1 13.2 %copy-start.24 = (f32[512,1024]{1,0:T(8,128)}, f32[512,1024]{1,0:T(8,128)S(1)}, u32[]{:S(2)}) copy-start(f32[512,1024]{1,0:T(8,128)S(1)} %get-tuple-element.1192) | copy-start | bytes 6291460
  245.1 13.2 %copy-start.73 = (f32[512]{0:T(512)}, f32[512]{0:T(512)S(1)}, u32[]{:S(2)}) copy-start(f32[512]{0:T(512)S(1)} %negate_multiply_fusion.4) | copy-start | bytes 6148
  258.4 9.7 copy-start.78
  271.9 3.6 copy-start.75
  281.7 370.9 %copy-start.47 = (s32[512]{0:T(512)S(1)}, s32[512]{0:T(512)}, u32[]{:S(2)}) copy-start(s32[512]{0:T(512)} %copy-done.46) | copy-start | bytes 6148
  292.3 8.6 copy-start.19
  294.7 6.2 copy-start.1
  333.8 68.2 %collective-permute-start.1 = (bf16[2,1,512,1024]{2,3,1,0:T(8,128)(2,1)}, bf16[2,1,512,1024]{2,3,1,0:T(8,128)(2,1)}, u32[]{:S(2)}, u32[]{:S(2)}) collective-permute-start(bf16[2,1,512,1024]{2,3,1,0:T(8,128)(2,1)} %convert_element_type.544), channel_id=1, source_target_pairs={{0,3},{1,0},{2,1},{3,2},{4,7},{5,4},{6,5},{7,6},{8,11},{9,8},{10,9... | collective-permute-start | bytes 6291464 | tf_op jit(solution)/shard_map/while/body/eval_jaxpr/ppermute | solution.py:18
  355.6 87.4 %collective-permute-start.2 = (bf16[2,1,512,1024]{2,3,1,0:T(8,128)(2,1)}, bf16[2,1,512,1024]{2,3,1,0:T(8,128)(2,1)}, u32[]{:S(2)}, u32[]{:S(2)}) collective-permute-start(bf16[2,1,512,1024]{2,3,1,0:T(8,128)(2,1)} %copy.100), channel_id=1, source_target_pairs={{0,3},{1,0},{2,1},{3,2},{4,7},{5,4},{6,5},{7,6},{8,11},{9,8},{10,9... | collective-permute-start | bytes 6291464 | tf_op jit(solution)/shard_map/while/body/eval_jaxpr/ppermute | solution.py:18
  457.0 49.8 %collective-permute-start.1 = (bf16[2,1,512,1024]{2,3,1,0:T(8,128)(2,1)}, bf16[2,1,512,1024]{2,3,1,0:T(8,128)(2,1)}, u32[]{:S(2)}, u32[]{:S(2)}) collective-permute-start(bf16[2,1,512,1024]{2,3,1,0:T(8,128)(2,1)} %convert_element_type.544), channel_id=1, source_target_pairs={{0,3},{1,0},{2,1},{3,2},{4,7},{5,4},{6,5},{7,6},{8,11},{9,8},{10,9... | collective-permute-start | bytes 6291464 | tf_op jit(solution)/shard_map/while/body/eval_jaxpr/ppermute | solution.py:18
  460.4 86.5 %collective-permute-start.2 = (bf16[2,1,512,1024]{2,3,1,0:T(8,128)(2,1)}, bf16[2,1,512,1024]{2,3,1,0:T(8,128)(2,1)}, u32[]{:S(2)}, u32[]{:S(2)}) collective-permute-start(bf16[2,1,512,1024]{2,3,1,0:T(8,128)(2,1)} %copy.100), channel_id=1, source_target_pairs={{0,3},{1,0},{2,1},{3,2},{4,7},{5,4},{6,5},{7,6},{8,11},{9,8},{10,9... | collective-permute-start | bytes 6291464 | tf_op jit(solution)/shard_map/while/body/eval_jaxpr/ppermute | solution.py:18
  560.9 49.8 %collective-permute-start.1 = (bf16[2,1,512,1024]{2,3,1,0:T(8,128)(2,1)}, bf16[2,1,512,1024]{2,3,1,0:T(8,128)(2,1)}, u32[]{:S(2)}, u32[]{:S(2)}) collective-permute-start(bf16[2,1,512,1024]{2,3,1,0:T(8,128)(2,1)} %convert_element_type.544), channel_id=1, source_target_pairs={{0,3},{1,0},{2,1},{3,2},{4,7},{5,4},{6,5},{7,6},{8,11},{9,8},{10,9... | collective-permute-start | bytes 6291464 | tf_op jit(solution)/shard_map/while/body/eval_jaxpr/ppermute | solution.py:18
  564.3 85.6 %collective-permute-start.2 = (bf16[2,1,512,1024]{2,3,1,0:T(8,128)(2,1)}, bf16[2,1,512,1024]{2,3,1,0:T(8,128)(2,1)}, u32[]{:S(2)}, u32[]{:S(2)}) collective-permute-start(bf16[2,1,512,1024]{2,3,1,0:T(8,128)(2,1)} %copy.100), channel_id=1, source_target_pairs={{0,3},{1,0},{2,1},{3,2},{4,7},{5,4},{6,5},{7,6},{8,11},{9,8},{10,9... | collective-permute-start | bytes 6291464 | tf_op jit(solution)/shard_map/while/body/eval_jaxpr/ppermute | solution.py:18
  654.0 4.2 copy-start.21
  654.0 47.7 %copy-start.25 = (f32[512,1024]{1,0:T(8,128)S(1)}, f32[512,1024]{1,0:T(8,128)}, u32[]{:S(2)}) copy-start(f32[512,1024]{1,0:T(8,128)} %copy-done.24) | copy-start | bytes 6291460
  654.0 47.7 %copy-start.74 = (f32[512]{0:T(512)S(1)}, f32[512]{0:T(512)}, u32[]{:S(2)}) copy-start(f32[512]{0:T(512)} %copy-done.73) | copy-start | bytes 6148
  658.2 53.7 %copy-start.9 = (f32[512,1024]{1,0:T(8,128)S(1)}, f32[512,1024]{1,0:T(8,128)}, u32[]{:S(2)}) copy-start(f32[512,1024]{1,0:T(8,128)} %copy-done.8) | copy-start | bytes 6291460
  658.2 53.7 %copy-start.54 = (f32[512]{0:T(512)S(1)}, f32[512]{0:T(512)}, u32[]{:S(2)}) copy-start(f32[512]{0:T(512)} %copy-done.53) | copy-start | bytes 6148
  658.2 53.7 %copy-start.63 = (f32[1,1024]{1,0:T(1,128)S(1)}, f32[1,1024]{1,0:T(1,128)}, u32[]{:S(2)}) copy-start(f32[1,1024]{1,0:T(1,128)} %get-tuple-element.1241) | copy-start | bytes 12292
  658.2 53.7 %copy-start.66 = (f32[512]{0:T(512)S(1)}, f32[512]{0:T(512)}, u32[]{:S(2)}) copy-start(f32[512]{0:T(512)} %copy-done.65) | copy-start | bytes 6148
  658.2 53.7 %copy-start.72 = (f32[1,1024]{1,0:T(1,128)S(1)}, f32[1,1024]{1,0:T(1,128)}, u32[]{:S(2)}) copy-start(f32[1,1024]{1,0:T(1,128)} %get-tuple-element.1245) | copy-start | bytes 12292
  658.2 53.7 %copy-start.79 = (bf16[512,4096]{1,0:T(8,128)(2,1)S(1)}, bf16[512,4096]{1,0:T(8,128)(2,1)}, u32[]{:S(2)}) copy-start(bf16[512,4096]{1,0:T(8,128)(2,1)} %copy-done.78) | copy-start | bytes 12582916
  658.2 83.1 %collective-permute-start.3 = (bf16[2,1,512,1024]{2,3,1,0:T(8,128)(2,1)}, bf16[2,1,512,1024]{2,3,1,0:T(8,128)(2,1)S(1)}, u32[]{:S(2)}, u32[]{:S(2)}) collective-permute-start(bf16[2,1,512,1024]{2,3,1,0:T(8,128)(2,1)} %convert_element_type.356), channel_id=1, source_target_pairs={{0,3},{1,0},{2,1},{3,2},{4,7},{5,4},{6,5},{7,6},{8,11},{9,8},{10,9... | collective-permute-start | bytes 6291464 | tf_op jit(solution)/shard_map/ppermute | solution.py:18
  727.4 7.7 copy-start.18
  727.4 7.7 copy-start.76
  739.3 2.3 copy-start.4
  739.3 2.3 copy-start.22
  739.3 2.3 copy-start.37
  739.3 2.4 copy-start.39
  741.4 15.4 %copy-start.15 = (bf16[2,1,512,1024]{2,3,1,0:T(8,128)(2,1)}, bf16[2,1,512,1024]{2,3,1,0:T(8,128)(2,1)S(1)}, u32[]{:S(2)}) copy-start(bf16[2,1,512,1024]{2,3,1,0:T(8,128)(2,1)S(1)} %collective-permute-done.3) | copy-start | bytes 6291460
  748.5 2.6 copy-start.7
  748.5 2.6 copy-start.41
  748.5 2.6 copy-start.44
  748.5 2.6 copy-start.50
  748.5 2.6 copy-start.70
  1017.7 18.5 %copy-start.16 = (bf16[2,1,512,1024]{2,3,1,0:T(8,128)(2,1)S(1)}, bf16[2,1,512,1024]{2,3,1,0:T(8,128)(2,1)}, u32[]{:S(2)}) copy-start(bf16[2,1,512,1024]{2,3,1,0:T(8,128)(2,1)} %copy-done.15) | copy-start | bytes 6291460
  1017.7 18.5 %copy-start.33 = (f32[512,1024]{1,0:T(8,128)S(1)}, f32[512,1024]{1,0:T(8,128)}, u32[]{:S(2)}) copy-start(f32[512,1024]{1,0:T(8,128)} %fusion.151) | copy-start | bytes 6291460
  1017.7 18.5 %copy-start.34 = (f32[512,1024]{1,0:T(8,128)S(1)}, f32[512,1024]{1,0:T(8,128)}, u32[]{:S(2)}) copy-start(f32[512,1024]{1,0:T(8,128)} %fusion.152) | copy-start | bytes 6291460
  1039.6 1.8 copy-start.56
  1039.6 1.8 copy-start.67
  1039.6 1.8 copy-start.55
  (20 other events, 28.1 us)
